TPU v7x, 128 devices: a whole 4x4x4 slice. The times are simulated.
128 devices in a mesh: row: 16 (over z_hi, x, core), col: 8 (over z_lo, y).
Axes of the slice: x: 4, y: 4, z: 4 (z_hi: 2, z_lo: 2; z = z_hi * 2 + z_lo), core: 2. Of those that a mesh axis runs over, the one named last changes fastest.
Arguments:
- doubles: bfloat16 [3600, 3840], P('row', 'col'), may hold values from -6 to 6
- singles: float32 [60, 480], replicated, may hold values from -3 to 3
- integrals: bfloat16 [3840, 32768], P(None, ('col', 'row')), may hold values from -0.09375 to 0.09375
Outputs:
- ladder: bfloat16 [3600, 32768], P('row', 'col')
All inputs are finite; a program needn't handle non-finite values.
Results may differ from a plain program's by a relative error of at most 0.005.
Values may be sent and summed in bfloat16 or wider, within the bound.
A program may use at most 128 MiB of HBM per device.

v0:
```python
import jax
import jax.numpy as jnp
from jax import lax
from jax.sharding import PartitionSpec as P


def onehot_rows(index, count):
    return (index[:, None] == jnp.arange(count, dtype=jnp.int32)[None, :]).astype(jnp.float32)


def build_tau(doubles, singles):
    pair_rows = doubles.shape[0]
    pair_cols = doubles.shape[1]
    occupied = singles.shape[0]
    virtual = singles.shape[1]
    global_row = lax.axis_index("row") * pair_rows + jnp.arange(pair_rows, dtype=jnp.int32)
    global_col = lax.axis_index("col") * pair_cols + jnp.arange(pair_cols, dtype=jnp.int32)
    first_occ = onehot_rows(global_row // occupied, occupied)
    second_occ = onehot_rows(global_row % occupied, occupied)
    first_vir = onehot_rows(global_col // virtual, virtual).T
    second_vir = onehot_rows(global_col % virtual, virtual).T
    exact = lax.Precision.HIGHEST
    left = jnp.dot(jnp.dot(first_occ, singles, precision=exact), first_vir, precision=exact)
    right = jnp.dot(jnp.dot(second_occ, singles, precision=exact), second_vir, precision=exact)
    return (doubles.astype(jnp.float32) + left * right).astype(jnp.bfloat16)


def on_device(doubles, singles, integrals):
    tau_local = build_tau(doubles, singles)
    tau_rows = lax.all_gather(tau_local, "col", axis=1, tiled=True)
    grid_block = lax.all_to_all(integrals, "row", split_axis=0, concat_axis=1, tiled=True)
    summed = jnp.dot(
        tau_rows,
        lax.all_gather(grid_block, "row", axis=0, tiled=True),
        preferred_element_type=jnp.float32,
    )
    return summed.astype(jnp.bfloat16)


def solution(mesh):
    in_specs = (P("row", "col"), P(), P(None, ("col", "row")))
    out_specs = P("row", "col")
    return jax.shard_map(
        on_device, mesh=mesh, in_specs=in_specs, out_specs=out_specs, check_vma=False
    )
```

profile of v0, /device:TPU:1, one launch (start us, length us, event | category | flops | bytes accessed | tf_op | source)
XLA Modules:
  0.0 266.1 jit_solution(14303256013045606890)
XLA Ops:
  6.5 0.0 copy-start
  6.5 0.0 copy-start.2
  6.5 0.0 copy-start.1
  6.5 0.0 all-gather.6.cloned.1.call-start
  6.6 0.8 copy-done
  7.4 0.4 fusion.7
  7.8 0.4 fusion.6
  8.2 0.7 fusion.3
  9.0 0.0 copy-done.2
  9.0 1.5 fusion.2
  10.4 0.0 all-gather.6.cloned.1.call-update
  10.5 0.0 all-gather.4.cloned.1.call-start
  10.5 0.0 copy-done.1
  10.5 51.3 %all_to_all.19 = bf16[16,240,256]{2,1,0:T(8,128)(2,1)S(1)} all-to-all(bf16[16,240,256]{2,1,0:T(8,128)(2,1)S(1)} %bitcast.18), channel_id=1, replica_groups=mesh['row'=16,'col'=8] {'row'}, dimensions={0} | all-to-all | bytes 3932160 | tf_op jit(solution)/shard_map/all_to_all | solution.py:31
  61.8 1.5 copy.8
  63.4 0.0 all-gather.4.cloned.1.call-update
  63.4 0.0 all-gather.6.cloned.1.call-done
  63.4 2.1 copy.6
  65.5 4.2 %reshape.40 = bf16[3840,225]{0,1:T(8,128)(2,1)} reshape(bf16[8,480,225]{1,0,2:T(8,128)(2,1)S(1)} %copy.6) | data formatting | bytes 3456000
  69.7 174.3 %all-gather.4.cloned.1.call-done = bf16[3840,4096]{1,0:T(8,128)(2,1)} async-done(((bf16[240,4096]{1,0:T(8,128)(2,1)}), bf16[3840,4096]{1,0:T(8,128)(2,1)}) %all-gather.4.cloned.1.call-update) | async-done | bytes 31457296 | tf_op jit(solution)/shard_map/all_gather | solution.py:34
  244.1 15.2 %convolution_convert_fusion = bf16[225,4096]{1,0:T(8,128)(2,1)} fusion(bf16[3840,225]{0,1:T(8,128)(2,1)} %reshape.40, bf16[3840,4096]{1,0:T(8,128)(2,1)} %all-gather.4.cloned.1.call-done), kind=kOutput, calls=%fused_computation | convolution fusion | flops 7078809600 | bytes 35028480 | tf_op jit(solution)/shard_map/dot_general | solution.py:32
  (2 shorter events, 0.0 us)
Async XLA Ops:
  6.5 0.9 copy-start
  6.5 2.4 copy-start.2
  6.5 4.0 %copy-start.1 = (bf16[3840,256]{1,0:T(8,128)(2,1)S(1)}, bf16[3840,256]{1,0:T(8,128)(2,1)}, u32[]{:S(2)}) copy-start(bf16[3840,256]{1,0:T(8,128)(2,1)} %param.5) | copy-start | bytes 5898244
  6.5 56.9 %all-gather.6.cloned.1.call-start = ((), (), s32[]{:S(2)}) async-start(), calls=%async_computation.2 | async-start | bytes 2138112 | tf_op jit(solution)/shard_map/all_gather | solution.py:30
  10.5 233.6 %all-gather.4.cloned.1.call-start = ((), (), s32[]{:S(2)}) async-start(), calls=%async_computation.1 | async-start | bytes 33423360 | tf_op jit(solution)/shard_map/all_gather | solution.py:34
Sparse Core Ops, SparseCore 0:
  10.6 48.8 all-gather.5
  63.5 180.5 all-gather.3
where the time goes:
time: 266 us
  waiting for transfers between devices  174 us (65%)
  blocking collectives  51.3 us (19%)
  matrix products  18.2 us (7%)
  between operations  13.5 us (5%)
  local copies, waits for them, and re-layouts  8.71 us (3%)
    all_gather x1, waiting for transfers between devices, on_device(): lax.all_gather(grid_block, 'row', axis=0, tiled=True)  174 us
    all_to_all x1, blocking collectives, on_device(): lax.all_to_all(integrals, 'row', split_axis=0, concat_axis=1, tiled=True)  51.3 us
    dot_general x1, matrix products, on_device(): jnp.dot(tau_rows, lax.all_gather(grid_block, 'row', axis=0, tiled=True),...  15.2 us
  transfers between devices with their start and end apart: 2, of which 1 were waited for; matrix products, arithmetic and copies ran while one was open for 3% of the time, Pallas kernels for 0%

commit v1 on v0

--- a/solution.py
+++ b/solution.py
@@ -2,6 +2,10 @@
 import jax.numpy as jnp
 from jax import lax
 from jax.sharding import PartitionSpec as P
+
+update_windows_here = lambda x_part: jnp.concatenate(
+    lax.all_to_all(jnp.stack([x_part for _ in range(lax.axis_size("row"))]), "row", 0, 0), axis=0
+)
 
 
 def onehot_rows(index, count):
@@ -29,11 +33,7 @@
     tau_local = build_tau(doubles, singles)
     tau_rows = lax.all_gather(tau_local, "col", axis=1, tiled=True)
     grid_block = lax.all_to_all(integrals, "row", split_axis=0, concat_axis=1, tiled=True)
-    summed = jnp.dot(
-        tau_rows,
-        lax.all_gather(grid_block, "row", axis=0, tiled=True),
-        preferred_element_type=jnp.float32,
-    )
+    summed = jnp.dot(tau_rows, update_windows_here(grid_block), preferred_element_type=jnp.float32)
     return summed.astype(jnp.bfloat16)
 
 

time: 266 us -> 525 us (1.97)
  waiting for transfers between devices: 174 us -> 433 us
  blocking collectives: 51.3 us -> 35.9 us
  local copies, waits for them, and re-layouts: 8.71 us -> 17.2 us
  starting transfers between devices: 0.04 us -> 6.66 us
    all_to_all x0 -> x1, waiting for transfers between devices: none -> 380 us  [lax.all_to_all(jnp.stack([x_part for _ in range(lax.axis_size('row'))]),...]
    all_gather x1 -> x0, waiting for transfers between devices: 174 us -> none  [on_device(): lax.all_gather(grid_block, 'row', axis=0, tiled=True)]
    all_gather x1, waiting for transfers between devices: 0.02 us -> 53.4 us  [on_device(): tau_rows = lax.all_gather(tau_local, 'col', axis=1, tiled=True)]
    all_to_all x1, blocking collectives: 51.3 us -> 35.9 us  [on_device(): lax.all_to_all(integrals, 'row', split_axis=0, concat_axis=1, tiled=True)]
    another operation x0 -> x2, local copies, waits for them, and re-layouts: none -> 10.8 us  [jnp.stack([x_part for _ in range(lax.axis_size('row'))])]
    all_to_all x0 -> x1, starting transfers between devices: none -> 6.62 us  [lax.all_to_all(jnp.stack([x_part for _ in range(lax.axis_size('row'))]),...]
  transfers between devices with their start and end apart: 2 -> 2, of which waited for: 1 -> 2; matrix products, arithmetic and copies ran while one was open for 3% -> 2% of each run, Pallas kernels for 0% -> 0%
where the time goes in v1:
time: 525 us
  waiting for transfers between devices  433 us (82%)
  blocking collectives  35.9 us (7%)
  matrix products  18.2 us (3%)
  local copies, waits for them, and re-layouts  17.2 us (3%)
  between operations  13.5 us (3%)
  starting transfers between devices  6.66 us (1%)
    all_to_all x1, waiting for transfers between devices, lax.all_to_all(jnp.stack([x_part for _ in range(lax.axis_size('row'))]),...  380 us
    all_gather x1, waiting for transfers between devices, on_device(): tau_rows = lax.all_gather(tau_local, 'col', axis=1, tiled=True)  53.4 us
    all_to_all x1, blocking collectives, on_device(): lax.all_to_all(integrals, 'row', split_axis=0, concat_axis=1, tiled=True)  35.9 us
    dot_general x1, matrix products, on_device(): jnp.dot(tau_rows, update_windows_here(grid_block), preferred_element_type...  15.2 us
    another operation x2, local copies, waits for them, and re-layouts, jnp.stack([x_part for _ in range(lax.axis_size('row'))])  10.8 us
  transfers between devices with their start and end apart: 2, of which 2 were waited for; matrix products, arithmetic and copies ran while one was open for 2% of the time, Pallas kernels for 0%

profile of v1, /device:TPU:1, one launch (start us, length us, event | category | flops | bytes accessed | tf_op | source)
XLA Modules:
  0.0 524.8 jit_solution(15253239911508701301)
XLA Ops:
  6.5 0.0 copy-start
  6.5 35.9 %all_to_all.21 = bf16[16,240,256]{2,1,0:T(8,128)(2,1)S(1)} all-to-all(bf16[16,240,256]{2,1,0:T(8,128)(2,1)} %bitcast.19), channel_id=1, replica_groups=mesh['row'=16,'col'=8] {'row'}, dimensions={0} | all-to-all | bytes 3932160 | tf_op jit(solution)/shard_map/all_to_all | solution.py:35
  42.4 0.2 copy.8
  42.7 10.6 %stack.5 = bf16[16,240,4096]{2,1,0:T(8,128)(2,1)} broadcast(bf16[240,4096]{1,0:T(8,128)(2,1)S(1)} %bitcast.17), dimensions={1,2} | broadcast | bytes 33423360 | tf_op jit(solution)/shard_map/stack | solution.py:7
  53.3 6.6 %all-to-all-start.1 = ((bf16[16,240,4096]{2,1,0:T(8,128)(2,1)}), bf16[16,240,4096]{2,1,0:T(8,128)(2,1)}, u32[]{:S(2)}, u32[]{:S(2)}) async-start(bf16[16,240,4096]{2,1,0:T(8,128)(2,1)} %stack.5), calls=%async_computation.1 | async-start | bytes 62914560 | tf_op jit(solution)/shard_map/all_to_all | solution.py:7
  59.9 0.0 copy-start.1
  59.9 0.0 all-gather.3.cloned.1.call-start
  60.0 0.0 copy-done
  60.0 0.4 fusion.7
  60.4 0.4 fusion.6
  60.8 0.7 fusion.3
  61.5 0.0 copy-done.1
  61.5 1.4 fusion.2
  63.0 0.0 all-gather.3.cloned.1.call-update
  63.0 53.4 %all-gather.3.cloned.1.call-done = bf16[8,480,225]{1,2,0:T(8,128)(2,1)} async-done(((bf16[1,480,225]{1,2,0:T(8,128)(2,1)}), bf16[8,480,225]{1,2,0:T(8,128)(2,1)}) %all-gather.3.cloned.1.call-update) | async-done | bytes 1728016 | tf_op jit(solution)/shard_map/all_gather | solution.py:34
  116.5 2.1 copy.6
  118.6 4.3 reshape.47
  122.8 379.9 %all-to-all-done.1 = bf16[16,240,4096]{2,1,0:T(8,128)(2,1)} async-done(((bf16[16,240,4096]{2,1,0:T(8,128)(2,1)}), bf16[16,240,4096]{2,1,0:T(8,128)(2,1)}, u32[]{:S(2)}, u32[]{:S(2)}) %all-to-all-start.1) | async-done | bytes 31457312 | tf_op jit(solution)/shard_map/all_to_all | solution.py:7
  502.7 15.2 %convolution_convert_fusion = bf16[225,4096]{1,0:T(8,128)(2,1)} fusion(bf16[3840,225]{0,1:T(8,128)(2,1)} %reshape.47, bf16[3840,4096]{1,0:T(8,128)(2,1)} %bitcast.4), kind=kOutput, calls=%fused_computation | convolution fusion | flops 7078809600 | bytes 35028480 | tf_op jit(solution)/shard_map/dot_general | solution.py:36
  (2 shorter events, 0.0 us)
Async XLA Ops:
  6.5 53.4 %copy-start = (f32[60,480]{1,0:T(8,128)S(1)}, f32[60,480]{1,0:T(8,128)}, u32[]{:S(2)}) copy-start(f32[60,480]{1,0:T(8,128)} %param.4) | copy-start | bytes 345604
  53.3 449.5 %all-to-all-start.1 = ((bf16[16,240,4096]{2,1,0:T(8,128)(2,1)}), bf16[16,240,4096]{2,1,0:T(8,128)(2,1)}, u32[]{:S(2)}, u32[]{:S(2)}) async-start(bf16[16,240,4096]{2,1,0:T(8,128)(2,1)} %stack.5), calls=%async_computation.1 | async-start | bytes 62914560 | tf_op jit(solution)/shard_map/all_to_all | solution.py:7
  59.9 1.7 copy-start.1
  59.9 56.6 %all-gather.3.cloned.1.call-start = ((), (), s32[]{:S(2)}) async-start(), calls=%async_computation.2 | async-start | bytes 2138112 | tf_op jit(solution)/shard_map/all_gather | solution.py:34
Sparse Core Ops, SparseCore 0:
  63.1 53.2 all-gather.2
